TPU v7x, 32 devices: a whole 2x2x4 slice. The times are simulated.
32 devices in a mesh: det: 8 (over z, x), tm: 4 (over y, core).
Axes of the slice: x: 2, y: 2, z: 4, core: 2. Of those that a mesh axis runs over, the one named last changes fastest.
Arguments:
- x_map: float32 [3, 4096, 256], P(None, ('det', 'tm')), may hold values from -6 to 6
- r_map: float32 [3, 4096, 256], P(None, ('det', 'tm')), may hold values from -45 to 45
- p_map: float32 [3, 4096, 256], P(None, ('det', 'tm')), may hold values from -45 to 45
- pointing: int32 [32, 16384], P('det', 'tm'), may hold values from 0 to 2047
- pol_angle: float32 [32, 16384], P('det', 'tm'), may hold values from -3.140625 to 3.140625
- noise_filter: bfloat16 [32, 8192], P('det'), may hold values from -2 to 2
- block_list: int32 [8, 128, 8], P('det', 'tm'), may hold values from 0 to 4095, as said below
- block_home: int32 [4096], replicated, may hold values from 0 to 4095, as said below
Outputs:
- x_next: float32 [3, 4096, 256], P(None, ('det', 'tm'))
- r_next: float32 [3, 4096, 256], P(None, ('det', 'tm'))
- p_next: float32 [3, 4096, 256], P(None, ('det', 'tm'))
Inputs may be any that keep to these rules, and one draw needn't show every extreme that they name: Block b is stored at row block_home[b] of the maps, a permutation. `block_list`: repeats allowed. The 256 entries of one device's lists name at most 16 blocks stored on any one device (counted with repeats), exactly 16 on some; one device's stored blocks are named 16 times by every device's lists.
All inputs are finite; a program needn't handle non-finite values.
Results may differ from a plain program's by a relative error of at most 0.0034.
The roundings to bfloat16 on the way count: a program that leaves them out, or rounds other values in their place, can miss the bound.
Values may be sent and summed in bfloat16 or wider, within the bound.
A program may use at most 128 MiB of HBM per device.

v0:
```python
import jax
import jax.numpy as jnp
from jax import lax
from jax.sharding import PartitionSpec as P


def with_halo(block, sides, width):
    for axis, dim in sides:
        count = lax.axis_size(axis)
        forward = [(i, i + 1) for i in range(count - 1)]
        backward = [(target, source) for source, target in forward]
        low = lax.ppermute(
            lax.slice_in_dim(block, block.shape[dim] - width, None, axis=dim), axis, forward
        )
        high = lax.ppermute(lax.slice_in_dim(block, 0, width, axis=dim), axis, backward)
        block = jnp.concatenate([low, block, high], axis=dim)
    return block


def apply_filter(padded, noise_filter, samples):
    tap_count = noise_filter.shape[1]
    window_len = tap_count + 128
    windows = samples // 128
    span_rows = tap_count // 128 + 1

    def one_detector(series, coeffs):
        extended = jnp.concatenate([coeffs, jnp.zeros((129,), coeffs.dtype)])
        toeplitz = jnp.tile(extended, 128)[: 128 * window_len].reshape(128, window_len)
        pieces = series.reshape(-1, 128)
        framed = jnp.stack(
            [pieces[offset_rows : offset_rows + windows] for offset_rows in range(span_rows)],
            axis=1,
        )
        framed = framed.reshape(windows, window_len)
        result = lax.dot_general(
            framed, toeplitz, (((1,), (1,)), ((), ())), preferred_element_type=jnp.float32
        )
        return result.reshape(samples)

    groups = padded.shape[0] // 4

    def one_group(bundle):
        return jax.vmap(one_detector)(bundle[0], bundle[1])

    output = lax.map(
        one_group, (padded.reshape(groups, 4, -1), noise_filter.reshape(groups, 4, tap_count))
    )
    return output.reshape(-1, samples)


def body(x_map, r_map, p_map, pointing, pol_angle, noise_filter, block_list, block_home):
    det_count = lax.axis_size("det")
    time_count = lax.axis_size("tm")
    devices = det_count * time_count
    list_len = block_list.shape[2]
    per_device = block_list.shape[1] * list_len
    capacity = 2 * per_device // devices
    slot_count = devices * capacity
    blocks_here = p_map.shape[1]
    pixels = p_map.shape[2]
    wanted = block_list.reshape(per_device)
    stored = jnp.take(block_home, wanted)
    owner_index = stored // blocks_here
    slot_of = stored % blocks_here
    member = (owner_index[:, None] == jnp.arange(devices, dtype=jnp.int32)[None, :]).astype(
        jnp.int32
    )
    ranking = jnp.sum((jnp.cumsum(member, axis=0) - 1) * member, axis=1)
    send_place = owner_index * capacity + ranking
    request = jnp.full((slot_count,), -1, jnp.int32).at[send_place].set(slot_of)
    asked_slots = lax.all_to_all(request, ("det", "tm"), split_axis=0, concat_axis=0, tiled=True)
    present = asked_slots >= 0
    answer = jnp.where(present[None, :, None], p_map[:, jnp.maximum(asked_slots, 0), :], 0.0)
    fetched = lax.all_to_all(answer, ("det", "tm"), split_axis=1, concat_axis=1, tiled=True)
    local_map = fetched[:, send_place, :].reshape(3, per_device * pixels)
    samples = pointing.shape[1]
    block_span = samples // block_list.shape[1]
    time_block = jnp.arange(samples, dtype=jnp.int32) // block_span
    address = time_block[None, :] * (list_len * pixels) + pointing
    cosine = jnp.cos(2.0 * pol_angle)
    sine_part = jnp.sin(2.0 * pol_angle)
    signal = (
        local_map[0][address] + cosine * local_map[1][address] + sine_part * local_map[2][address]
    ).astype(jnp.bfloat16)
    tap_count = noise_filter.shape[1]
    padded = with_halo(signal, (("tm", 1),), tap_count // 2)
    rounded = apply_filter(padded, noise_filter, samples).astype(jnp.bfloat16)
    filtered = lax.optimization_barrier(rounded).astype(jnp.float32)
    terms = jnp.stack([filtered, filtered * cosine, filtered * sine_part]).reshape(3, -1)
    partial_value = (
        jnp.zeros((3, per_device * pixels), jnp.float32).at[:, address.reshape(-1)].add(terms)
    )
    outgoing = (
        jnp.zeros((3, slot_count, pixels), jnp.float32)
        .at[:, send_place, :]
        .set(partial_value.reshape(3, per_device, pixels))
    )
    returned = lax.all_to_all(outgoing, ("det", "tm"), split_axis=1, concat_axis=1, tiled=True)
    selector = (asked_slots[:, None] == jnp.arange(blocks_here, dtype=jnp.int32)[None, :]).astype(
        jnp.float32
    )
    image = jnp.einsum("sk,csb->ckb", selector, returned, precision=lax.Precision.HIGHEST)
    norm_old = lax.psum(jnp.sum(r_map * r_map), ("det", "tm"))
    curvature = lax.psum(jnp.sum(p_map * image), ("det", "tm"))
    step_size = norm_old / curvature
    r_next = r_map - step_size * image
    norm_new = lax.psum(jnp.sum(r_next * r_next), ("det", "tm"))
    x_next = x_map + step_size * p_map
    p_next = r_next + norm_new / norm_old * p_map
    return (x_next, r_next, p_next)


def solution(mesh):
    return jax.shard_map(
        body,
        mesh=mesh,
        in_specs=(
            P(None, ("det", "tm"), None),
            P(None, ("det", "tm"), None),
            P(None, ("det", "tm"), None),
            P("det", "tm"),
            P("det", "tm"),
            P("det", None),
            P("det", "tm", None),
            P(),
        ),
        out_specs=(
            P(None, ("det", "tm"), None),
            P(None, ("det", "tm"), None),
            P(None, ("det", "tm"), None),
        ),
        check_vma=False,
    )
```

profile of v0, /device:TPU:0, one launch (start us, length us, event | category | flops | bytes accessed | tf_op | source)
XLA Modules:
  0.0 697.4 jit_solution(10474817990767673283)
XLA Ops:
  6.0 14.2 %all_to_all.22 = s32[32,16,1]{1,2,0:T(1,128)S(1)} all-to-all(s32[32,16,1]{1,2,0:T(1,128)S(1)} %bitcast.432), channel_id=1, replica_groups=mesh['det'=8,'tm'=4] {'det','tm'}, dimensions={0} | all-to-all | bytes 4096 | tf_op jit(solution)/shard_map/all_to_all | solution.py:71
  22.2 3.7 gather_fusion.1
  26.0 2.4 copy.112
  28.5 2.9 all-to-all-start.1
  32.8 47.3 %all-to-all-done.1 = f32[3,512,256]{2,0,1:T(4,128)S(1)} async-done(((f32[3,512,256]{2,0,1:T(4,128)}), f32[3,512,256]{2,0,1:T(4,128)S(1)}, u32[]{:S(2)}, u32[]{:S(2)}) %all-to-all-start.1) | async-done | bytes 1572896 | tf_op jit(solution)/shard_map/all_to_all | solution.py:74
  81.9 90.8 %gather_fusion.3 = f32[16384]{0:T(1024)S(1)} fusion(f32[65536]{0:T(1024)S(1)} %bitcast.354, s32[16384]{0:T(1024)} %broadcast_clamp_fusion), kind=kCustom, calls=%fused_computation.3 | custom fusion | bytes 196608 | tf_op jit(solution)/shard_map/gather | solution.py:83
  172.8 90.5 %gather_fusion.4 = f32[16384]{0:T(1024)S(1)} fusion(f32[65536]{0:T(1024)S(1)} %bitcast.353, s32[16384]{0:T(1024)S(1)} %copy-done.5), kind=kCustom, calls=%fused_computation.4 | custom fusion | bytes 196608 | tf_op jit(solution)/shard_map/gather | solution.py:83
  263.4 90.5 %gather_fusion.5 = f32[16384]{0:T(1024)S(1)} fusion(f32[65536]{0:T(1024)S(1)} %bitcast.352, s32[16384]{0:T(1024)S(1)} %copy-done.5), kind=kCustom, calls=%fused_computation.5 | custom fusion | bytes 196608 | tf_op jit(solution)/shard_map/gather | solution.py:83
  357.9 3.9 tile.14
  361.8 18.0 %reshape.389 = bf16[4260352]{0:T(1024)(128)(2,1)} reshape(bf16[4,128,8321]{2,1,0:T(8,128)(2,1)} %tile.14) | data formatting | bytes 17041408
  379.7 15.0 %tile.15 = bf16[4,1065088]{1,0:T(4,128)(2,1)} reshape(bf16[4260352]{0:T(1024)(128)(2,1)} %reshape.389) | data formatting | bytes 17041408 | tf_op jit(solution)/shard_map/while/body/eval_jaxpr/vmap()/tile | solution.py:28
  396.2 1.9 slice-done
  398.1 3.0 fusion.17
  402.1 5.2 copy.114
  407.3 100.8 %scatter_custom_fusion.1 = f32[3,65536]{0,1:T(8,128)} fusion(s32[16384]{0:T(1024)S(1)} %bitcast.431, f32[16384,3]{1,0:T(8,128)} %copy.114, f32[]{:T(128)} %constant.81.clone.1), kind=kCustom, calls=%fused_computation.9 | custom fusion | flops 49152 | bytes 786944 | tf_op jit(solution)/shard_map/scatter-add | solution.py:91
  508.1 17.9 %copy.115 = f32[3,256,256]{2,0,1:T(4,128)S(1)} copy(f32[3,256,256]{0,2,1:T(8,128)} %bitcast.355) | data formatting | bytes 1572864 | tf_op jit(solution)/shard_map/reshape | solution.py:96
  527.7 24.0 %scatter_fusion = f32[3,512,256]{2,0,1:T(4,128)} fusion(f32[3,512,256]{2,0,1:T(4,128)} %broadcast_in_dim.31, s32[256]{0:T(256)S(1)} %bitcast.436, f32[256,3,256]{2,1,0:T(4,128)S(1)} %bitcast.422), kind=kCustom, calls=%fused_computation.8 | custom fusion | bytes 2360320 | tf_op jit(solution)/shard_map/scatter | solution.py:96
  551.6 6.7 all-to-all-start.2
  559.4 1.9 copy.119
  562.0 45.1 %all-to-all-done.2 = f32[3,512,256]{2,0,1:T(4,128)S(1)} async-done(((f32[3,512,256]{2,0,1:T(4,128)}), f32[3,512,256]{2,0,1:T(4,128)S(1)}, u32[]{:S(2)}, u32[]{:S(2)}) %all-to-all-start.2) | async-done | bytes 1572896 | tf_op jit(solution)/shard_map/all_to_all | solution.py:98
  607.1 2.9 multiply_reduce_fusion.1
  610.0 38.4 %all-reduce.1 = (f32[]{:T(128)}, f32[]{:T(128)}) all-reduce(f32[]{:T(128)} %multiply_reduce_fusion.2, f32[]{:T(128)} %get-tuple-element.41), channel_id=1, replica_groups=mesh['det'=8,'tm'=4] {'det','tm'}, use_global_device_ids=true, to_apply=%region_1.2 | all-reduce | flops 2 | bytes 16 | tf_op jit(solution)/shard_map/psum | solution.py:103
  649.6 1.9 multiply_reduce_fusion
  651.6 41.4 %psum.23 = f32[]{:T(128)} all-reduce(f32[]{:T(128)} %get-tuple-element.28), channel_id=1, replica_groups=mesh['det'=8,'tm'=4] {'det','tm'}, use_global_device_ids=true, to_apply=%region_11.12 | all-reduce | flops 1 | bytes 8 | tf_op jit(solution)/shard_map/psum | solution.py:107
  (155 shorter events, 23.1 us)
Async XLA Ops:
  0.6 1.1 copy-start
  0.6 21.5 %copy-start.2 = (f32[3,128,256]{2,1,0:T(8,128)S(1)}, f32[3,128,256]{2,1,0:T(8,128)}, u32[]{:S(2)}) copy-start(f32[3,128,256]{2,1,0:T(8,128)} %param.10) | copy-start | bytes 1179652
  4.5 27.6 %copy-start.12 = (s32[256,1]{0,1:T(1,128)}, s32[256,1]{0,1:T(1,128)S(1)}, u32[]{:S(2)}) copy-start(s32[256,1]{0,1:T(1,128)S(1)} %compare_select_fusion.2) | copy-start | bytes 3076
  21.6 0.6 copy-start.10
  28.5 2.9 copy-start.8
  28.5 51.6 %all-to-all-start.1 = ((f32[3,512,256]{2,0,1:T(4,128)}), f32[3,512,256]{2,0,1:T(4,128)S(1)}, u32[]{:S(2)}, u32[]{:S(2)}) async-start(f32[3,512,256]{2,0,1:T(4,128)} %copy.112), calls=%async_computation.1 | async-start | bytes 4194304 | tf_op jit(solution)/shard_map/all_to_all | solution.py:74
  81.9 90.8 %copy-start.5 = (s32[16384]{0:T(1024)S(1)}, s32[16384]{0:T(1024)}, u32[]{:S(2)}) copy-start(s32[16384]{0:T(1024)} %broadcast_clamp_fusion) | copy-start | bytes 196612
  263.3 90.6 %copy-start.6 = (f32[4,4096]{1,0:T(4,128)S(1)}, f32[4,4096]{1,0:T(4,128)}, u32[]{:S(2)}) copy-start(f32[4,4096]{1,0:T(4,128)} %param.12) | copy-start | bytes 196612
  263.3 94.4 %copy-start.7 = (s32[1,1,4,4096]{3,1,2,0:T(1,128)S(1)}, s32[1,1,4,4096]{3,1,2,0:T(1,128)}, u32[]{:S(2)}) copy-start(s32[1,1,4,4096]{3,1,2,0:T(1,128)} %copy.127) | copy-start | bytes 196612
  263.4 94.5 %copy-start.9 = (bf16[4,8192]{1,0:T(4,128)(2,1)S(1)}, bf16[4,8192]{1,0:T(4,128)(2,1)}, u32[]{:S(2)}) copy-start(bf16[4,8192]{1,0:T(4,128)(2,1)} %param.13) | copy-start | bytes 196612
  354.5 40.2 %collective-permute-start = (bf16[4,4096]{1,0:T(4,128)(2,1)S(1)}, bf16[4,4096]{1,0:T(4,128)(2,1)S(1)}, u32[]{:S(2)}, u32[]{:S(2)}) collective-permute-start(bf16[4,4096]{1,0:T(4,128)(2,1)S(1)} %add_convert_fusion), channel_id=1, source_target_pairs={{0,1},{1,2},{2,3},{4,5},{5,6},{6,7},{8,9},{9,10},{10,11},{12,13},{... | collective-permute-start | bytes 98312 | tf_op jit(solution)/shard_map/ppermute | solution.py:12
  356.0 38.7 %collective-permute-start.1 = (bf16[4,4096]{1,0:T(4,128)(2,1)S(1)}, bf16[4,4096]{1,0:T(4,128)(2,1)S(1)}, u32[]{:S(2)}, u32[]{:S(2)}) collective-permute-start(bf16[4,4096]{1,0:T(4,128)(2,1)S(1)} %add_convert_fusion), channel_id=1, source_target_pairs={{1,0},{2,1},{3,2},{5,4},{6,5},{7,6},{9,8},{10,9},{11,10},{13,12},{... | collective-permute-start | bytes 98312 | tf_op jit(solution)/shard_map/ppermute | solution.py:15
  394.7 3.4 slice-start
  508.1 19.6 %copy-start.13 = (s32[256,1]{0,1:T(1,128)S(1)}, s32[256,1]{0,1:T(1,128)}, u32[]{:S(2)}) copy-start(s32[256,1]{0,1:T(1,128)} %copy-done.12) | copy-start | bytes 3076
  551.6 6.9 copy-start.3
  551.6 55.5 %all-to-all-start.2 = ((f32[3,512,256]{2,0,1:T(4,128)}), f32[3,512,256]{2,0,1:T(4,128)S(1)}, u32[]{:S(2)}, u32[]{:S(2)}) async-start(f32[3,512,256]{2,0,1:T(4,128)} %scatter_fusion), calls=%async_computation.2 | async-start | bytes 4194304 | tf_op jit(solution)/shard_map/all_to_all | solution.py:98
  558.3 48.8 %copy-start.11 = (s32[512]{0:T(512)S(1)}, s32[512]{0:T(512)}, u32[]{:S(2)}) copy-start(s32[512]{0:T(512)} %copy-done.10) | copy-start | bytes 6148
  562.0 133.2 %copy-start.4 = (f32[3,128,256]{1,2,0:T(8,128)S(1)}, f32[3,128,256]{1,2,0:T(8,128)}, u32[]{:S(2)}) copy-start(f32[3,128,256]{1,2,0:T(8,128)} %copy.119) | copy-start | bytes 1179652
  694.3 2.8 copy-start.1
where the time goes:
time: 706 us; the launch traced here: 697 us
  local copies, waits for them, and re-layouts  381 us (54%)
  other arithmetic  107 us (15%)
  blocking collectives  94.1 us (13%)
  waiting for transfers between devices  92.4 us (13%)
  starting transfers between devices  12.8 us (2%)
    scatter-add x1, other arithmetic, body(): jnp.zeros((3, per_device * pixels), jnp.float32).at[:, address.reshape(-1)]  101 us
    gather x2, local copies, waits for them, and re-layouts, body(): local_map[0][address] + cosine * local_map[1][address]  90.8 us
    gather x2, local copies, waits for them, and re-layouts, body(): local_map[1][address]  90.6 us
    gather x2, local copies, waits for them, and re-layouts, body(): local_map[2][address]  90.6 us
    all_to_all x1, waiting for transfers between devices, body(): lax.all_to_all(answer, ('det', 'tm'), split_axis=1, concat_axis=1, tiled=...  47.3 us
    all_to_all x1, waiting for transfers between devices, body(): lax.all_to_all(outgoing, ('det', 'tm'), split_axis=1, concat_axis=1, tile...  45.1 us
    psum x1, blocking collectives, body(): norm_new = lax.psum(jnp.sum(r_next * r_next), ('det', 'tm'))  41.4 us
    psum x1, blocking collectives, body(): norm_old = lax.psum(jnp.sum(r_map * r_map), ('det', 'tm'))  38.4 us
  transfers between devices with their start and end apart: 4, of which 2 were waited for; matrix products, arithmetic and copies ran while one was open for 6% of the time, Pallas kernels for 0%

commit v1 on v0

--- a/solution.py
+++ b/solution.py
@@ -95,7 +95,11 @@
         .at[:, send_place, :]
         .set(partial_value.reshape(3, per_device, pixels))
     )
-    returned = lax.all_to_all(outgoing, ("det", "tm"), split_axis=1, concat_axis=1, tiled=True)
+    val = jax.lax.psum(1, ("det", "tm"))
+    response = jnp.split(outgoing, val, axis=1)
+    out_arr = jnp.stack(response)
+    tmp = jax.lax.all_to_all(out_arr, ("det", "tm"), 0, 0)
+    returned = jnp.concatenate(tmp, axis=1)
     selector = (asked_slots[:, None] == jnp.arange(blocks_here, dtype=jnp.int32)[None, :]).astype(
         jnp.float32
     )

time: 706 us -> 676 us (0.958)
  local copies, waits for them, and re-layouts: 381 us -> 363 us
  waiting for transfers between devices: 92.4 us -> 82.6 us
    scatter x1, local copies, waits for them, and re-layouts: 24 us -> 6.93 us  [body(): outgoing = jnp.zeros((3, slot_count, pixels), jnp.float32).at[:, send_pla...]
    all_to_all x1, waiting for transfers between devices: 45.1 us -> 35.3 us  [body(): tmp = jax.lax.all_to_all(out_arr, ('det', 'tm'), 0, 0)]
    unnamed x107 -> x136, local copies, waits for them, and re-layouts: 27.3 us -> 26.4 us
where the time goes in v1:
time: 676 us; the launch traced here: 668 us
  local copies, waits for them, and re-layouts  363 us (54%)
  other arithmetic  106 us (16%)
  blocking collectives  94 us (14%)
  waiting for transfers between devices  82.6 us (12%)
  starting transfers between devices  12.9 us (2%)
    scatter-add x1, other arithmetic, body(): jnp.zeros((3, per_device * pixels), jnp.float32).at[:, address.reshape(-1)]  101 us
    gather x2, local copies, waits for them, and re-layouts, body(): local_map[0][address] + cosine * local_map[1][address]  90.8 us
    gather x2, local copies, waits for them, and re-layouts, body(): local_map[1][address]  90.6 us
    gather x2, local copies, waits for them, and re-layouts, body(): local_map[2][address]  90.6 us
    all_to_all x1, waiting for transfers between devices, body(): lax.all_to_all(answer, ('det', 'tm'), split_axis=1, concat_axis=1, tiled=...  47.3 us
    psum x1, blocking collectives, body(): norm_new = lax.psum(jnp.sum(r_next * r_next), ('det', 'tm'))  41.6 us
    psum x1, blocking collectives, body(): norm_old = lax.psum(jnp.sum(r_map * r_map), ('det', 'tm'))  38.1 us
    all_to_all x1, waiting for transfers between devices, body(): tmp = jax.lax.all_to_all(out_arr, ('det', 'tm'), 0, 0)  35.3 us
  transfers between devices with their start and end apart: 4, of which 2 were waited for; matrix products, arithmetic and copies ran while one was open for 6% of the time, Pallas kernels for 0%

profile of v1, /device:TPU:0, one launch (start us, length us, event | category | flops | bytes accessed | tf_op | source)
XLA Modules:
  0.0 668.2 jit_solution(6447239565400551168)
XLA Ops:
  1.8 1.7 gather_fusion
  6.0 14.2 %all_to_all.22 = s32[32,16,1]{1,2,0:T(1,128)S(1)} all-to-all(s32[32,16,1]{1,2,0:T(1,128)S(1)} %bitcast.565), channel_id=1, replica_groups=mesh['det'=8,'tm'=4] {'det','tm'}, dimensions={0} | all-to-all | bytes 4096 | tf_op jit(solution)/shard_map/all_to_all | solution.py:71
  22.2 3.7 gather_fusion.1
  26.0 2.4 copy.113
  28.5 2.9 all-to-all-start.1
  32.7 47.3 %all-to-all-done.1 = f32[3,512,256]{2,0,1:T(4,128)S(1)} async-done(((f32[3,512,256]{2,0,1:T(4,128)}), f32[3,512,256]{2,0,1:T(4,128)S(1)}, u32[]{:S(2)}, u32[]{:S(2)}) %all-to-all-start.1) | async-done | bytes 1572896 | tf_op jit(solution)/shard_map/all_to_all | solution.py:74
  81.9 90.8 %gather_fusion.3 = f32[16384]{0:T(1024)S(1)} fusion(f32[65536]{0:T(1024)S(1)} %bitcast.486, s32[16384]{0:T(1024)} %broadcast_clamp_fusion), kind=kCustom, calls=%fused_computation.3 | custom fusion | bytes 196608 | tf_op jit(solution)/shard_map/gather | solution.py:83
  172.7 90.5 %gather_fusion.4 = f32[16384]{0:T(1024)S(1)} fusion(f32[65536]{0:T(1024)S(1)} %bitcast.485, s32[16384]{0:T(1024)S(1)} %copy-done.4), kind=kCustom, calls=%fused_computation.4 | custom fusion | bytes 196608 | tf_op jit(solution)/shard_map/gather | solution.py:83
  263.4 90.5 %gather_fusion.5 = f32[16384]{0:T(1024)S(1)} fusion(f32[65536]{0:T(1024)S(1)} %bitcast.484, s32[16384]{0:T(1024)S(1)} %copy-done.4), kind=kCustom, calls=%fused_computation.5 | custom fusion | bytes 196608 | tf_op jit(solution)/shard_map/gather | solution.py:83
  356.0 1.8 collective-permute-start.1
  357.9 3.9 tile.14
  361.7 18.0 %reshape.397 = bf16[4260352]{0:T(1024)(128)(2,1)} reshape(bf16[4,128,8321]{2,1,0:T(8,128)(2,1)} %tile.14) | data formatting | bytes 17041408
  379.7 15.0 %tile.15 = bf16[4,1065088]{1,0:T(4,128)(2,1)} reshape(bf16[4260352]{0:T(1024)(128)(2,1)} %reshape.397) | data formatting | bytes 17041408 | tf_op jit(solution)/shard_map/while/body/eval_jaxpr/vmap()/tile | solution.py:28
  396.2 1.9 slice-done
  398.1 3.0 fusion.12
  402.1 5.2 copy.115
  407.3 100.8 %scatter_custom_fusion.1 = f32[3,65536]{0,1:T(8,128)} fusion(s32[16384]{0:T(1024)S(1)} %bitcast.564, f32[16384,3]{1,0:T(8,128)} %copy.115, f32[]{:T(128)} %constant.81.clone.1), kind=kCustom, calls=%fused_computation.9 | custom fusion | flops 49152 | bytes 786944 | tf_op jit(solution)/shard_map/scatter-add | solution.py:91
  508.1 17.9 %copy.116 = f32[3,256,256]{2,0,1:T(4,128)S(1)} copy(f32[3,256,256]{0,2,1:T(8,128)} %bitcast.487) | data formatting | bytes 1572864 | tf_op jit(solution)/shard_map/reshape | solution.py:96
  526.3 6.9 %scatter_fusion = f32[3,512,256]{2,0,1:T(4,128)S(1)} fusion(f32[3,512,256]{2,0,1:T(4,128)S(1)} %broadcast_in_dim.31, s32[256]{0:T(256)S(1)} %bitcast.569, f32[256,3,256]{2,1,0:T(4,128)S(1)} %bitcast.555), kind=kCustom, calls=%fused_computation.8 | custom fusion | bytes 2360320 | tf_op jit(solution)/shard_map/scatter | solution.py:96
  535.5 6.7 %all-to-all-start.2 = ((f32[32,3,16,256]{3,2,1,0:T(8,128)}), f32[32,3,16,256]{3,2,1,0:T(8,128)S(1)}, u32[]{:S(2)}, u32[]{:S(2)}) async-start(f32[32,3,16,256]{3,2,1,0:T(8,128)} %copy.117), calls=%async_computation.2 | async-start | bytes 3145728 | tf_op jit(solution)/shard_map/all_to_all | solution.py:101
  544.4 35.3 %all-to-all-done.2 = f32[32,3,16,256]{3,2,1,0:T(8,128)S(1)} async-done(((f32[32,3,16,256]{3,2,1,0:T(8,128)}), f32[32,3,16,256]{3,2,1,0:T(8,128)S(1)}, u32[]{:S(2)}, u32[]{:S(2)}) %all-to-all-start.2) | async-done | bytes 1572896 | tf_op jit(solution)/shard_map/all_to_all | solution.py:101
  579.9 2.1 multiply_reduce_fusion.1
  582.0 38.1 %all-reduce.1 = (f32[]{:T(128)}, f32[]{:T(128)}) all-reduce(f32[]{:T(128)} %multiply_reduce_fusion.2, f32[]{:T(128)} %get-tuple-element.41), channel_id=1, replica_groups=mesh['det'=8,'tm'=4] {'det','tm'}, use_global_device_ids=true, to_apply=%region_1.2 | all-reduce | flops 2 | bytes 16 | tf_op jit(solution)/shard_map/psum | solution.py:107
  622.1 41.6 %psum.23 = f32[]{:T(128)} all-reduce(f32[]{:T(128)} %get-tuple-element.28), channel_id=1, replica_groups=mesh['det'=8,'tm'=4] {'det','tm'}, use_global_device_ids=true, to_apply=%region_11.12 | all-reduce | flops 1 | bytes 8 | tf_op jit(solution)/shard_map/psum | solution.py:111
  (187 shorter events, 21.5 us)
Async XLA Ops:
  0.6 1.1 copy-start
  0.6 21.5 %copy-start.2 = (f32[3,128,256]{2,1,0:T(8,128)S(1)}, f32[3,128,256]{2,1,0:T(8,128)}, u32[]{:S(2)}) copy-start(f32[3,128,256]{2,1,0:T(8,128)} %param.10) | copy-start | bytes 1179652
  4.5 27.6 %copy-start.11 = (s32[256,1]{0,1:T(1,128)}, s32[256,1]{0,1:T(1,128)S(1)}, u32[]{:S(2)}) copy-start(s32[256,1]{0,1:T(1,128)S(1)} %compare_select_fusion.2) | copy-start | bytes 3076
  21.6 0.6 copy-start.9
  28.5 2.9 copy-start.7
  28.5 51.6 %all-to-all-start.1 = ((f32[3,512,256]{2,0,1:T(4,128)}), f32[3,512,256]{2,0,1:T(4,128)S(1)}, u32[]{:S(2)}, u32[]{:S(2)}) async-start(f32[3,512,256]{2,0,1:T(4,128)} %copy.113), calls=%async_computation.1 | async-start | bytes 4194304 | tf_op jit(solution)/shard_map/all_to_all | solution.py:74
  81.9 90.8 %copy-start.4 = (s32[16384]{0:T(1024)S(1)}, s32[16384]{0:T(1024)}, u32[]{:S(2)}) copy-start(s32[16384]{0:T(1024)} %broadcast_clamp_fusion) | copy-start | bytes 196612
  263.3 90.6 %copy-start.5 = (f32[4,4096]{1,0:T(4,128)S(1)}, f32[4,4096]{1,0:T(4,128)}, u32[]{:S(2)}) copy-start(f32[4,4096]{1,0:T(4,128)} %param.12) | copy-start | bytes 196612
  263.3 94.4 %copy-start.6 = (s32[1,1,4,4096]{3,1,2,0:T(1,128)S(1)}, s32[1,1,4,4096]{3,1,2,0:T(1,128)}, u32[]{:S(2)}) copy-start(s32[1,1,4,4096]{3,1,2,0:T(1,128)} %copy.131) | copy-start | bytes 196612
  263.3 94.5 %copy-start.8 = (bf16[4,8192]{1,0:T(4,128)(2,1)S(1)}, bf16[4,8192]{1,0:T(4,128)(2,1)}, u32[]{:S(2)}) copy-start(bf16[4,8192]{1,0:T(4,128)(2,1)} %param.13) | copy-start | bytes 196612
  354.4 40.2 %collective-permute-start = (bf16[4,4096]{1,0:T(4,128)(2,1)S(1)}, bf16[4,4096]{1,0:T(4,128)(2,1)S(1)}, u32[]{:S(2)}, u32[]{:S(2)}) collective-permute-start(bf16[4,4096]{1,0:T(4,128)(2,1)S(1)} %add_convert_fusion), channel_id=1, source_target_pairs={{0,1},{1,2},{2,3},{4,5},{5,6},{6,7},{8,9},{9,10},{10,11},{12,13},{... | collective-permute-start | bytes 98312 | tf_op jit(solution)/shard_map/ppermute | solution.py:12
  356.0 38.7 %collective-permute-start.1 = (bf16[4,4096]{1,0:T(4,128)(2,1)S(1)}, bf16[4,4096]{1,0:T(4,128)(2,1)S(1)}, u32[]{:S(2)}, u32[]{:S(2)}) collective-permute-start(bf16[4,4096]{1,0:T(4,128)(2,1)S(1)} %add_convert_fusion), channel_id=1, source_target_pairs={{1,0},{2,1},{3,2},{5,4},{6,5},{7,6},{9,8},{10,9},{11,10},{13,12},{... | collective-permute-start | bytes 98312 | tf_op jit(solution)/shard_map/ppermute | solution.py:15
  394.7 3.4 slice-start
  508.1 18.2 %copy-start.12 = (s32[256,1]{0,1:T(1,128)S(1)}, s32[256,1]{0,1:T(1,128)}, u32[]{:S(2)}) copy-start(s32[256,1]{0,1:T(1,128)} %copy-done.11) | copy-start | bytes 3076
  535.5 6.9 %copy-start.3 = (f32[3,128,256]{2,1,0:T(8,128)S(1)}, f32[3,128,256]{2,1,0:T(8,128)}, u32[]{:S(2)}) copy-start(f32[3,128,256]{2,1,0:T(8,128)} %param.9) | copy-start | bytes 1179652
  535.5 44.2 %all-to-all-start.2 = ((f32[32,3,16,256]{3,2,1,0:T(8,128)}), f32[32,3,16,256]{3,2,1,0:T(8,128)S(1)}, u32[]{:S(2)}, u32[]{:S(2)}) async-start(f32[32,3,16,256]{3,2,1,0:T(8,128)} %copy.117), calls=%async_computation.2 | async-start | bytes 3145728 | tf_op jit(solution)/shard_map/all_to_all | solution.py:101
  542.5 37.3 %copy-start.10 = (s32[512]{0:T(512)S(1)}, s32[512]{0:T(512)}, u32[]{:S(2)}) copy-start(s32[512]{0:T(512)} %copy-done.9) | copy-start | bytes 6148
  665.1 2.8 copy-start.1
